TPU v7x, 32 devices: a whole 2x2x4 slice. The times are simulated.
32 devices in a mesh: grp: 4 (over z), head: 8 (over y, x, core).
Axes of the slice: x: 2, y: 2, z: 4, core: 2. Of those that a mesh axis runs over, the one named last changes fastest.
Arguments:
- queries: bfloat16 [8, 8, 4096], P('head'), may hold values from -1500 to 1500
- shared_prefix_keys: bfloat16 [8, 512, 512], P('head', 'grp'), may hold values from -6 to 6
- shared_prefix_values: bfloat16 [8, 512, 512], P('head', 'grp'), may hold values from -6 to 6
- row_suffix_keys: bfloat16 [8, 8, 16, 512], P('head', 'grp'), may hold values from -6 to 6
- row_suffix_values: bfloat16 [8, 8, 16, 512], P('head', 'grp'), may hold values from -6 to 6
- suffix_lengths: int32 [8, 8], P('head', 'grp'), may hold values from 1 to 16, as said below
- residual: bfloat16 [8, 8, 2048], P('head', 'grp'), may hold values from -4 to 4
- out_weight: bfloat16 [4096, 2048], P('head'), may hold values from -0.5 to 0.5
- norm_gain: float32 [2048], replicated, may hold values from 0.5 to 2
- router_weight: bfloat16 [2048, 16], replicated, may hold values from -0.125 to 0.125
- gate_weights: bfloat16 [16, 2048, 384], P('head'), may hold values from -0.125 to 0.125
- up_weights: bfloat16 [16, 2048, 384], P('head'), may hold values from -0.125 to 0.125
- down_weights: bfloat16 [16, 384, 2048], P('head'), may hold values from -0.3125 to 0.3125
- expert_ids: int32 [8, 8, 8], P('head', 'grp'), may hold values from 0 to 15, all different within a row; in each aligned block of 2 rows (0 to 1, 2 to 3, ..., all dimensions but the last counted through in order) at most 2 rows name the same one
Outputs:
- layer_out: float32 [8, 8, 2048], P('head', 'grp')
Inputs may be any that keep to these rules, and one draw needn't show every extreme that they name: `expert_ids`: each row names 8 different experts; in each aligned block of 2 rows (the rows of one device, prompts then rows in order) no expert is named by more than 2 rows, a bound that some block reaches. `suffix_lengths`: every prompt has a row whose suffix holds 16 tokens.
All inputs are finite; a program needn't handle non-finite values.
Results may differ from a plain program's by a relative error of at most 0.007.
Values may be sent and summed in bfloat16 or wider, within the bound.
A program may use at most 128 MiB of HBM per device.

v0:
```python
import math

import jax
import jax.numpy as jnp
from jax import lax
from jax.sharding import PartitionSpec as P

QUERY_HEADS = 32
KEY_VALUE_HEADS = 4
HEAD_SIZE = 128
TOPK = 8


masked_score = -1e30
norm_epsilon = 1e-06


def join_states(earlier_state, later_state):
    peak_one, mass_one, sum_one = earlier_state
    peak_two, mass_two, sum_two = later_state
    joint_peak = jnp.maximum(peak_one, peak_two)
    keep_first = jnp.exp(peak_one - joint_peak)
    keep_second = jnp.exp(peak_two - joint_peak)
    return (
        joint_peak,
        mass_one * keep_first + mass_two * keep_second,
        sum_one * keep_first[..., None] + sum_two * keep_second[..., None],
    )


def shards(
    queries,
    shared_prefix_keys,
    shared_prefix_values,
    row_suffix_keys,
    row_suffix_values,
    suffix_lengths,
    residual,
    out_weight,
    norm_gain,
    router_weight,
    gate_weights,
    up_weights,
    down_weights,
    expert_ids,
):
    group_count = lax.axis_size("grp")
    head_count = lax.axis_size("head")
    row_block = lax.axis_index("grp")
    every_row = queries.shape[1]
    prompt_own_rows = residual.shape[1]
    query_group_width = QUERY_HEADS // KEY_VALUE_HEADS
    score_scale = 1.0 / math.sqrt(HEAD_SIZE)
    heads_of_queries = queries[0].reshape(every_row, KEY_VALUE_HEADS, query_group_width, HEAD_SIZE)
    local_keys = shared_prefix_keys[0].reshape(-1, KEY_VALUE_HEADS, HEAD_SIZE)
    local_values = shared_prefix_values[0].reshape(-1, KEY_VALUE_HEADS, HEAD_SIZE)
    scores = (
        jnp.einsum(
            "rkgd,pkd->rkgp", heads_of_queries, local_keys, preferred_element_type=jnp.float32
        )
        * score_scale
    )
    row_peak = jnp.max(scores, -1)
    expo_terms = jnp.exp(scores - row_peak[..., None])
    total_mass = jnp.sum(expo_terms, -1)
    weighted = jnp.einsum(
        "rkgp,pkd->rkgd",
        expo_terms.astype(jnp.bfloat16),
        local_values,
        preferred_element_type=jnp.float32,
    )
    start_row = row_block * prompt_own_rows
    own_queries = lax.dynamic_slice_in_dim(heads_of_queries, start_row, prompt_own_rows, 0)
    suffix_key_rows = row_suffix_keys[0].reshape(prompt_own_rows, -1, KEY_VALUE_HEADS, HEAD_SIZE)
    suffix_value_rows = row_suffix_values[0].reshape(
        prompt_own_rows, -1, KEY_VALUE_HEADS, HEAD_SIZE
    )
    suf_count = suffix_key_rows.shape[1]
    in_suffix = (jnp.arange(suf_count)[None, :] < suffix_lengths[0][:, None])[:, None, None, :]
    suf_scores = (
        jnp.einsum(
            "rkgd,rskd->rkgs", own_queries, suffix_key_rows, preferred_element_type=jnp.float32
        )
        * score_scale
    )
    suf_scores = jnp.where(in_suffix, suf_scores, masked_score)
    suf_peak = jnp.max(suf_scores, -1)
    suf_terms = jnp.where(in_suffix, jnp.exp(suf_scores - suf_peak[..., None]), 0.0)
    suf_mass = jnp.sum(suf_terms, -1)
    suf_weighted = jnp.einsum(
        "rkgs,rskd->rkgd",
        suf_terms.astype(jnp.bfloat16),
        suffix_value_rows,
        preferred_element_type=jnp.float32,
    )
    own_state = (
        lax.dynamic_slice_in_dim(row_peak, start_row, prompt_own_rows, 0),
        lax.dynamic_slice_in_dim(total_mass, start_row, prompt_own_rows, 0),
        lax.dynamic_slice_in_dim(weighted, start_row, prompt_own_rows, 0),
    )
    own_peak, own_mass, own_weighted = join_states(own_state, (suf_peak, suf_mass, suf_weighted))
    row_peak = lax.dynamic_update_slice_in_dim(row_peak, own_peak, start_row, 0).reshape(
        every_row, QUERY_HEADS
    )
    total_mass = lax.dynamic_update_slice_in_dim(total_mass, own_mass, start_row, 0).reshape(
        every_row, QUERY_HEADS
    )
    weighted = lax.dynamic_update_slice_in_dim(weighted, own_weighted, start_row, 0).reshape(
        every_row, QUERY_HEADS, HEAD_SIZE
    )
    peak_parts = row_peak.reshape(1, group_count, prompt_own_rows, QUERY_HEADS)
    mass_parts = total_mass.reshape(1, group_count, prompt_own_rows, QUERY_HEADS)
    weighted_parts = weighted.reshape(1, group_count, prompt_own_rows, QUERY_HEADS, HEAD_SIZE)
    got_peak, got_mass, got_weighted = (
        lax.all_to_all(
            lax.all_to_all(peak_parts, "grp", split_axis=1, concat_axis=1, tiled=True),
            "head",
            split_axis=3,
            concat_axis=0,
            tiled=True,
        ),
        lax.all_to_all(
            lax.all_to_all(mass_parts, "grp", split_axis=1, concat_axis=1, tiled=True),
            "head",
            split_axis=3,
            concat_axis=0,
            tiled=True,
        ),
        lax.all_to_all(
            lax.all_to_all(weighted_parts, "grp", split_axis=1, concat_axis=1, tiled=True),
            "head",
            split_axis=3,
            concat_axis=0,
            tiled=True,
        ),
    )
    best_peak = jnp.max(got_peak, 1)
    factors = jnp.exp(got_peak - best_peak[:, None])
    joined_mass = jnp.sum(got_mass * factors, 1)
    joined_weighted = jnp.sum(got_weighted * factors[..., None], 1)
    mine = (joined_weighted / joined_mass[..., None]).astype(jnp.bfloat16)
    flat_attn = mine.reshape(head_count * prompt_own_rows, -1)
    projected = lax.psum_scatter(
        jnp.dot(flat_attn, out_weight, preferred_element_type=jnp.float32),
        "head",
        scatter_dimension=0,
        tiled=True,
    )
    hidden_state = residual[0].astype(jnp.float32) + projected
    mean_square = jnp.mean(hidden_state * hidden_state, -1, keepdims=True)
    normed = (hidden_state * lax.rsqrt(mean_square + norm_epsilon) * norm_gain).astype(jnp.bfloat16)
    logits = jnp.dot(normed, router_weight, preferred_element_type=jnp.float32)
    experts_all = router_weight.shape[1]
    capacity = max(2, prompt_own_rows * TOPK * 2 // experts_all)
    chosen_ids = expert_ids[0]
    is_chosen = chosen_ids[..., None] == jnp.arange(experts_all, dtype=jnp.int32)
    chosen_logits = jnp.sum(jnp.where(is_chosen, logits[:, None, :], 0.0), -1)
    chosen_expo = jnp.exp(chosen_logits)
    route_weights = chosen_expo / jnp.sum(chosen_expo, -1, keepdims=True)
    flat_match = is_chosen.reshape(prompt_own_rows * TOPK, experts_all).astype(jnp.int32)
    earlier = jnp.cumsum(flat_match, 0) - flat_match
    slot_index = jnp.sum(earlier * flat_match, -1).reshape(prompt_own_rows, TOPK)
    target_slot = chosen_ids * capacity + slot_index
    place_map = jnp.any(
        target_slot[..., None] == jnp.arange(experts_all * capacity, dtype=jnp.int32), 1
    ).astype(jnp.bfloat16)
    buffer = jnp.einsum("rs,rd->sd", place_map, normed, preferred_element_type=jnp.float32).astype(
        jnp.bfloat16
    )
    buffer = buffer.reshape(head_count, -1, buffer.shape[1])
    arrived = lax.all_to_all(buffer, "head", split_axis=0, concat_axis=0, tiled=True)
    local_experts = gate_weights.shape[0]
    arrived = arrived.reshape(head_count, local_experts, capacity, -1)
    gate_out = jnp.einsum(
        "secd,edf->secf", arrived, gate_weights, preferred_element_type=jnp.float32
    )
    up_out = jnp.einsum("secd,edf->secf", arrived, up_weights, preferred_element_type=jnp.float32)
    inner_act = (jax.nn.silu(gate_out) * up_out).astype(jnp.bfloat16)
    produced = jnp.einsum(
        "secf,efd->secd", inner_act, down_weights, preferred_element_type=jnp.float32
    ).astype(jnp.bfloat16)
    produced = produced.reshape(head_count, local_experts * capacity, -1)
    returned = lax.all_to_all(produced, "head", split_axis=0, concat_axis=0, tiled=True)
    returned = returned.reshape(experts_all * capacity, -1)
    gathered = (
        returned[target_slot.reshape(-1)].reshape(prompt_own_rows, TOPK, -1).astype(jnp.float32)
    )
    routed_sum = jnp.sum(route_weights[..., None] * gathered, 1)
    layer_out = hidden_state + routed_sum
    return layer_out[None]


def solution(mesh):
    return jax.shard_map(
        shards,
        mesh=mesh,
        in_specs=(
            P("head", None, None),
            P("head", "grp", None),
            P("head", "grp", None),
            P("head", "grp", None, None),
            P("head", "grp", None, None),
            P("head", "grp"),
            P("head", "grp", None),
            P("head", None),
            P(),
            P(),
            P("head", None, None),
            P("head", None, None),
            P("head", None, None),
            P("head", "grp", None),
        ),
        out_specs=P("head", "grp", None),
        check_vma=False,
    )
```

profile of v0, /device:TPU:0, one launch (start us, length us, event | category | flops | bytes accessed | tf_op | source)
XLA Modules:
  0.0 165.0 jit_solution(2216354133994578624)
XLA Ops:
  6.5 1.6 copy.185
  9.4 1.4 reshape_squeeze.18
  16.6 1.3 fusion.57
  18.6 6.3 %all-to-all-start.2 = ((f32[1,4,2,32]{3,2,0,1:T(2,128)}), f32[1,4,2,32]{3,2,0,1:T(2,128)S(1)}, u32[]{:S(2)}, u32[]{:S(2)}) async-start(f32[1,4,2,32]{3,2,0,1:T(2,128)} %bitcast.12), calls=%async_computation.2 | async-start | bytes 8192 | tf_op jit(solution)/shard_map/all_to_all | solution.py:116
  28.4 2.1 %all-to-all-done.2 = f32[1,4,2,32]{3,2,0,1:T(2,128)S(1)} async-done(((f32[1,4,2,32]{3,2,0,1:T(2,128)}), f32[1,4,2,32]{3,2,0,1:T(2,128)S(1)}, u32[]{:S(2)}, u32[]{:S(2)}) %all-to-all-start.2) | async-done | bytes 1056 | tf_op jit(solution)/shard_map/all_to_all | solution.py:116
  30.5 3.2 %all-to-all-start.4 = ((f32[1,4,2,32]{3,2,0,1:T(2,128)}), f32[1,4,2,32]{3,2,0,1:T(2,128)S(1)}, u32[]{:S(2)}, u32[]{:S(2)}) async-start(f32[1,4,2,32]{3,2,0,1:T(2,128)} %bitcast.16), calls=%async_computation.4 | async-start | bytes 8192 | tf_op jit(solution)/shard_map/all_to_all | solution.py:123
  35.1 4.2 %all-to-all-done.4 = f32[1,4,2,32]{3,2,0,1:T(2,128)S(1)} async-done(((f32[1,4,2,32]{3,2,0,1:T(2,128)}), f32[1,4,2,32]{3,2,0,1:T(2,128)S(1)}, u32[]{:S(2)}, u32[]{:S(2)}) %all-to-all-start.4) | async-done | bytes 1056 | tf_op jit(solution)/shard_map/all_to_all | solution.py:123
  39.3 3.7 %all-to-all-start.3 = ((f32[1,4,2,32]{1,2,0,3:T(2,128)}), f32[1,4,2,32]{1,2,0,3:T(2,128)S(1)}, u32[]{:S(2)}, u32[]{:S(2)}) async-start(f32[1,4,2,32]{1,2,0,3:T(2,128)} %copy.117), calls=%async_computation.3 | async-start | bytes 65536 | tf_op jit(solution)/shard_map/all_to_all | solution.py:115
  44.5 3.4 %all-to-all-done.3 = f32[1,4,2,32]{1,2,0,3:T(2,128)S(1)} async-done(((f32[1,4,2,32]{1,2,0,3:T(2,128)}), f32[1,4,2,32]{1,2,0,3:T(2,128)S(1)}, u32[]{:S(2)}, u32[]{:S(2)}) %all-to-all-start.3) | async-done | bytes 1056 | tf_op jit(solution)/shard_map/all_to_all | solution.py:115
  47.8 3.3 %all-to-all-start.5 = ((f32[1,4,2,32]{1,2,0,3:T(2,128)}), f32[1,4,2,32]{1,2,0,3:T(2,128)S(1)}, u32[]{:S(2)}, u32[]{:S(2)}) async-start(f32[1,4,2,32]{1,2,0,3:T(2,128)} %copy.122), calls=%async_computation.5 | async-start | bytes 65536 | tf_op jit(solution)/shard_map/all_to_all | solution.py:122
  53.7 2.2 %all-to-all-done.5 = f32[1,4,2,32]{1,2,0,3:T(2,128)S(1)} async-done(((f32[1,4,2,32]{1,2,0,3:T(2,128)}), f32[1,4,2,32]{1,2,0,3:T(2,128)S(1)}, u32[]{:S(2)}, u32[]{:S(2)}) %all-to-all-start.5) | async-done | bytes 1056 | tf_op jit(solution)/shard_map/all_to_all | solution.py:122
  55.9 3.3 %all-to-all-start = ((f32[1,4,2,32,128]{4,3,2,0,1:T(8,128)}), f32[1,4,2,32,128]{4,3,2,0,1:T(8,128)S(1)}, u32[]{:S(2)}, u32[]{:S(2)}) async-start(f32[1,4,2,32,128]{4,3,2,0,1:T(8,128)} %bitcast.8), calls=%async_computation | async-start | bytes 262144 | tf_op jit(solution)/shard_map/all_to_all | solution.py:130
  59.8 5.5 %all-to-all-done = f32[1,4,2,32,128]{4,3,2,0,1:T(8,128)S(1)} async-done(((f32[1,4,2,32,128]{4,3,2,0,1:T(8,128)}), f32[1,4,2,32,128]{4,3,2,0,1:T(8,128)S(1)}, u32[]{:S(2)}, u32[]{:S(2)}) %all-to-all-start) | async-done | bytes 131104 | tf_op jit(solution)/shard_map/all_to_all | solution.py:130
  66.1 3.4 %all-to-all-start.1 = ((f32[1,4,2,32,128]{4,2,1,0,3:T(2,128)}), f32[1,4,2,32,128]{4,2,1,0,3:T(2,128)S(1)}, u32[]{:S(2)}, u32[]{:S(2)}) async-start(f32[1,4,2,32,128]{4,2,1,0,3:T(2,128)} %copy.113), calls=%async_computation.1 | async-start | bytes 262144 | tf_op jit(solution)/shard_map/all_to_all | solution.py:129
  69.5 5.4 %all-to-all-done.1 = f32[1,4,2,32,128]{4,2,1,0,3:T(2,128)S(1)} async-done(((f32[1,4,2,32,128]{4,2,1,0,3:T(2,128)}), f32[1,4,2,32,128]{4,2,1,0,3:T(2,128)S(1)}, u32[]{:S(2)}, u32[]{:S(2)}) %all-to-all-start.1) | async-done | bytes 131104 | tf_op jit(solution)/shard_map/all_to_all | solution.py:129
  75.2 2.6 %fusion.49 = f32[16,2048]{1,0:T(8,128)} fusion(bf16[512,2048]{1,0:T(8,128)(2,1)} %param.21, bf16[2,8,4,128]{3,2,1,0:T(4,128)(2,1)S(1)} %bitcast.138), kind=kOutput, calls=%fused_computation.51 | convolution fusion | flops 33554432 | bytes 2244608 | tf_op jit(solution)/shard_map/dot_general | solution.py:144
  77.8 50.4 %all-reduce.3.cloned.1.call-done = f32[16,2048]{1,0:T(8,128)} async-done(((f32[16,2048]{1,0:T(8,128)}), f32[16,2048]{1,0:T(8,128)}) %all-reduce.3.cloned.1.call-update) | async-done | bytes 131088
  132.1 3.4 %all-to-all-start.6 = ((bf16[8,4,2048]{2,1,0:T(4,128)(2,1)}), bf16[8,4,2048]{2,1,0:T(4,128)(2,1)S(1)}, u32[]{:S(2)}, u32[]{:S(2)}) async-start(bf16[8,4,2048]{2,1,0:T(4,128)(2,1)} %reshape.132), calls=%async_computation.6 | async-start | bytes 262144 | tf_op jit(solution)/shard_map/all_to_all | solution.py:171
  135.8 5.2 %all-to-all-done.6 = bf16[8,4,2048]{2,1,0:T(4,128)(2,1)S(1)} async-done(((bf16[8,4,2048]{2,1,0:T(4,128)(2,1)}), bf16[8,4,2048]{2,1,0:T(4,128)(2,1)S(1)}, u32[]{:S(2)}, u32[]{:S(2)}) %all-to-all-start.6) | async-done | bytes 131104 | tf_op jit(solution)/shard_map/all_to_all | solution.py:171
  141.0 2.4 %fusion.10 = f32[8,2,2,384]{3,0,2,1:T(8,128)S(1)} fusion(bf16[8,2,2,2048]{3,0,2,1:T(8,128)(2,1)S(1)} %bitcast.126, bf16[2,2048,384]{2,1,0:T(8,128)(2,1)} %param.24), kind=kOutput, calls=%fused_computation.11 | convolution fusion | flops 50331648 | bytes 3325952 | tf_op jit(solution)/shard_map/secd,edf->secf/dot_general | solution.py:174
  143.5 2.8 %fusion.6 = bf16[2,8,2,2048]{3,1,2,0:T(8,128)(2,1)S(1)} fusion(bf16[2,384,2048]{2,1,0:T(8,128)(2,1)S(1)} %copy-done, bf16[8,2,2,2048]{3,0,2,1:T(8,128)(2,1)S(1)} %bitcast.127, bf16[2,2048,384]{2,1,0:T(8,128)(2,1)} %param.25, f32[8,2,2,384]{3,0,2,1:T(8,128)S(1)} %fusion.10), kind=kOutput, calls=%fused_computation.7 | convolution fusion | flops 100802560 | bytes 6602752 | tf_op jit(solution)/shard_map/secf,efd->secd/dot_general | solution.py:179
  147.1 3.4 %all-to-all-start.7 = ((bf16[8,4,2048]{2,1,0:T(4,128)(2,1)}), bf16[8,4,2048]{2,1,0:T(4,128)(2,1)S(1)}, u32[]{:S(2)}, u32[]{:S(2)}) async-start(bf16[8,4,2048]{2,1,0:T(4,128)(2,1)} %copy.126), calls=%async_computation.7 | async-start | bytes 262144 | tf_op jit(solution)/shard_map/all_to_all | solution.py:183
  150.5 5.4 %all-to-all-done.7 = bf16[8,4,2048]{2,1,0:T(4,128)(2,1)S(1)} async-done(((bf16[8,4,2048]{2,1,0:T(4,128)(2,1)}), bf16[8,4,2048]{2,1,0:T(4,128)(2,1)S(1)}, u32[]{:S(2)}, u32[]{:S(2)}) %all-to-all-start.7) | async-done | bytes 131104 | tf_op jit(solution)/shard_map/all_to_all | solution.py:183
  156.7 1.5 add_bitcast_fusion
  (60 shorter events, 23.2 us)
Async XLA Ops:
  6.5 136.9 %copy-start = (bf16[2,384,2048]{2,1,0:T(8,128)(2,1)S(1)}, bf16[2,384,2048]{2,1,0:T(8,128)(2,1)}, u32[]{:S(2)}) copy-start(bf16[2,384,2048]{2,1,0:T(8,128)(2,1)} %param.26) | copy-start | bytes 9437188
  14.8 120.7 %copy-start.2 = (s32[1,2,8]{2,1,0:T(2,128)S(1)}, s32[1,2,8]{2,1,0:T(2,128)}, u32[]{:S(2)}) copy-start(s32[1,2,8]{2,1,0:T(2,128)} %param.27) | copy-start | bytes 196
  18.6 11.9 %all-to-all-start.2 = ((f32[1,4,2,32]{3,2,0,1:T(2,128)}), f32[1,4,2,32]{3,2,0,1:T(2,128)S(1)}, u32[]{:S(2)}, u32[]{:S(2)}) async-start(f32[1,4,2,32]{3,2,0,1:T(2,128)} %bitcast.12), calls=%async_computation.2 | async-start | bytes 8192 | tf_op jit(solution)/shard_map/all_to_all | solution.py:116
  30.5 8.8 %all-to-all-start.4 = ((f32[1,4,2,32]{3,2,0,1:T(2,128)}), f32[1,4,2,32]{3,2,0,1:T(2,128)S(1)}, u32[]{:S(2)}, u32[]{:S(2)}) async-start(f32[1,4,2,32]{3,2,0,1:T(2,128)} %bitcast.16), calls=%async_computation.4 | async-start | bytes 8192 | tf_op jit(solution)/shard_map/all_to_all | solution.py:123
  39.3 8.6 %all-to-all-start.3 = ((f32[1,4,2,32]{1,2,0,3:T(2,128)}), f32[1,4,2,32]{1,2,0,3:T(2,128)S(1)}, u32[]{:S(2)}, u32[]{:S(2)}) async-start(f32[1,4,2,32]{1,2,0,3:T(2,128)} %copy.117), calls=%async_computation.3 | async-start | bytes 65536 | tf_op jit(solution)/shard_map/all_to_all | solution.py:115
  47.8 8.1 %all-to-all-start.5 = ((f32[1,4,2,32]{1,2,0,3:T(2,128)}), f32[1,4,2,32]{1,2,0,3:T(2,128)S(1)}, u32[]{:S(2)}, u32[]{:S(2)}) async-start(f32[1,4,2,32]{1,2,0,3:T(2,128)} %copy.122), calls=%async_computation.5 | async-start | bytes 65536 | tf_op jit(solution)/shard_map/all_to_all | solution.py:122
  55.9 9.4 %all-to-all-start = ((f32[1,4,2,32,128]{4,3,2,0,1:T(8,128)}), f32[1,4,2,32,128]{4,3,2,0,1:T(8,128)S(1)}, u32[]{:S(2)}, u32[]{:S(2)}) async-start(f32[1,4,2,32,128]{4,3,2,0,1:T(8,128)} %bitcast.8), calls=%async_computation | async-start | bytes 262144 | tf_op jit(solution)/shard_map/all_to_all | solution.py:130
  66.1 8.8 %all-to-all-start.1 = ((f32[1,4,2,32,128]{4,2,1,0,3:T(2,128)}), f32[1,4,2,32,128]{4,2,1,0,3:T(2,128)S(1)}, u32[]{:S(2)}, u32[]{:S(2)}) async-start(f32[1,4,2,32,128]{4,2,1,0,3:T(2,128)} %copy.113), calls=%async_computation.1 | async-start | bytes 262144 | tf_op jit(solution)/shard_map/all_to_all | solution.py:129
  69.4 58.8 %all-reduce.3.cloned.1.call-start = ((), (), s32[]{:S(2)}) async-start(), calls=%async_computation.8 | async-start | bytes 262144
  132.1 8.8 %all-to-all-start.6 = ((bf16[8,4,2048]{2,1,0:T(4,128)(2,1)}), bf16[8,4,2048]{2,1,0:T(4,128)(2,1)S(1)}, u32[]{:S(2)}, u32[]{:S(2)}) async-start(bf16[8,4,2048]{2,1,0:T(4,128)(2,1)} %reshape.132), calls=%async_computation.6 | async-start | bytes 262144 | tf_op jit(solution)/shard_map/all_to_all | solution.py:171
  143.5 13.2 %copy-start.1 = (bf16[1,2,2048]{2,1,0:T(2,128)(2,1)S(1)}, bf16[1,2,2048]{2,1,0:T(2,128)(2,1)}, u32[]{:S(2)}) copy-start(bf16[1,2,2048]{2,1,0:T(2,128)(2,1)} %param.20) | copy-start | bytes 24580
  147.1 8.8 %all-to-all-start.7 = ((bf16[8,4,2048]{2,1,0:T(4,128)(2,1)}), bf16[8,4,2048]{2,1,0:T(4,128)(2,1)S(1)}, u32[]{:S(2)}, u32[]{:S(2)}) async-start(bf16[8,4,2048]{2,1,0:T(4,128)(2,1)} %copy.126), calls=%async_computation.7 | async-start | bytes 262144 | tf_op jit(solution)/shard_map/all_to_all | solution.py:183
Sparse Core Ops, SparseCore 0:
  78.0 50.2 all-reduce.2
where the time goes:
time: 166 us; the launch traced here: 165 us
  waiting for transfers between devices  83.8 us (50%)
  starting transfers between devices  30.1 us (18%)
  local copies, waits for them, and re-layouts  15.3 us (9%)
  between operations  14.3 us (9%)
  matrix products  11.5 us (7%)
  other arithmetic  10 us (6%)
    unnamed x2, waiting for transfers between devices  50.5 us
    all_to_all x1, starting transfers between devices, shards(): lax.all_to_all(peak_parts, 'grp', split_axis=1, concat_axis=1, tiled=True)  6.32 us
    all_to_all x1, waiting for transfers between devices, shards(): lax.all_to_all(weighted_parts, 'grp', split_axis=1, concat_axis=1, tiled=...  5.53 us
    all_to_all x1, waiting for transfers between devices, shards(): lax.all_to_all(produced, 'head', split_axis=0, concat_axis=0, tiled=True)  5.39 us
    all_to_all x1, waiting for transfers between devices, shards(): lax.all_to_all(lax.all_to_all(weighted_parts, 'grp', split_axis=1, concat...  5.39 us
    all_to_all x1, waiting for transfers between devices, shards(): lax.all_to_all(buffer, 'head', split_axis=0, concat_axis=0, tiled=True)  5.18 us
    all_to_all x1, waiting for transfers between devices, shards(): lax.all_to_all(mass_parts, 'grp', split_axis=1, concat_axis=1, tiled=True)  4.16 us
    all_to_all x1, starting transfers between devices, shards(): lax.all_to_all(lax.all_to_all(peak_parts, 'grp', split_axis=1, concat_axi...  3.72 us
  transfers between devices with their start and end apart: 9, of which 9 were waited for; matrix products, arithmetic and copies ran while one was open for 5% of the time, Pallas kernels for 0%

commit v1 on v0

v1 whole, which is shorter than its diff:
```python
import functools
import math

import jax
import jax.numpy as jnp
from jax import lax
from jax.experimental import pallas as pl
from jax.experimental.pallas import tpu as pltpu
from jax.sharding import PartitionSpec as P

QUERY_HEADS = 32
KEY_VALUE_HEADS = 4
HEAD_SIZE = 128
TOPK = 8

masked_score = -1e30
norm_epsilon = 1e-06
f32, bf16, i32 = jnp.float32, jnp.bfloat16, jnp.int32
MESH = pl.DeviceIdType.MESH


def dot(a, b):
    return jnp.dot(a, b, preferred_element_type=f32)


def dot_nt(a, b):
    return lax.dot_general(a, b, (((1,), (1,)), ((), ())), preferred_element_type=f32)


def one_hot(shape, source):
    a = lax.broadcasted_iota(i32, shape, 0)
    b = lax.broadcasted_iota(i32, shape, 1)
    col = lax.broadcasted_iota(i32, shape, 2)
    hit = jnp.where(source(a, b) == col, 1.0, 0.0).astype(f32)
    return hit.reshape(shape[0] * shape[1], shape[2]).astype(bf16)


def kernel(
    G,
    H,
    q_hbm,
    k_hbm,
    v_hbm,
    sk_hbm,
    sv_hbm,
    len_hbm,
    res_hbm,
    ow_hbm,
    gain_hbm,
    rw_hbm,
    gw_hbm,
    uw_hbm,
    dw_hbm,
    ids_hbm,
    out_ref,
    q_ref,
    k_ref,
    v_ref,
    sk_ref,
    sv_ref,
    len_ref,
    res_ref,
    ow_ref,
    gain_ref,
    rw_ref,
    gw_ref,
    uw_ref,
    dw_ref,
    ids_ref,
    s1,
    r1,
    s2,
    r2,
    s3,
    r3,
    s4,
    r4,
    gain_cr,
    res_cr,
    load_sem,
    send_sem,
    recv_sem,
):
    N = G * H
    g = lax.axis_index("grp")
    h = lax.axis_index("head")
    me = h * G + g

    rows = q_ref.shape[1]
    own = res_ref.shape[1]
    width = res_ref.shape[2]
    suffix = sk_ref.shape[2]
    group = QUERY_HEADS // KEY_VALUE_HEADS
    heads_dev = QUERY_HEADS // H
    per_group = group // heads_dev
    slot_rows = s1.shape[1] // 2
    chunks, chunk_width = 16 // own, s2.shape[2]
    all_rows = H * own
    local_experts = gw_ref.shape[0]
    experts = rw_ref.shape[1]

    pairs = [
        (q_hbm, q_ref),
        (k_hbm, k_ref),
        (len_hbm, len_ref),
        (sk_hbm, sk_ref),
        (v_hbm, v_ref),
        (sv_hbm, sv_ref),
        (res_hbm, res_ref),
        (gain_hbm, gain_ref),
        (ids_hbm, ids_ref),
        (ow_hbm, ow_ref),
        (rw_hbm, rw_ref),
        (gw_hbm, gw_ref),
        (uw_hbm, uw_ref),
        (dw_hbm, dw_ref),
    ]
    loads = [pltpu.make_async_copy(a, b, load_sem.at[i]) for i, (a, b) in enumerate(pairs)]
    for load in loads:
        load.start()

    barrier = pltpu.get_barrier_semaphore()

    def greet(i, carry):
        d = lax.rem(me + i, N)
        pl.semaphore_signal(
            barrier, inc=1, device_id=(lax.rem(d, G), lax.div(d, G)), device_id_type=MESH
        )
        return carry

    lax.fori_loop(1, N, greet, 0)

    def query_source(a, b):
        if per_group == 1:
            head_block, block = 0, a
        else:
            head_block, block = lax.div(a, G), lax.rem(a, G)
        head, row = lax.div(b, own), lax.rem(b, own)
        found = (head_block * heads_dev + head) * rows + block * own + row
        return jnp.where(b < heads_dev * own, found, -1)

    to_slots = one_hot((per_group * G, slot_rows, group * rows), query_source)
    to_heads = one_hot(
        (heads_dev, all_rows, H * slot_rows),
        lambda a, b: lax.div(b, own) * slot_rows + a * own + lax.rem(b, own),
    )
    to_owner = one_hot(
        (H, 16, chunks * all_rows),
        lambda a, b: lax.div(b, own) * all_rows + a * own + lax.rem(b, own),
    )
    to_chunks = one_hot(
        (chunks, all_rows, H * 16),
        lambda a, b: lax.div(b, own) * 16 + a * own + lax.rem(b, own),
    )
    stat_row = lax.broadcasted_iota(i32, (HEAD_SIZE, 2 * HEAD_SIZE), 0)
    stat_col = lax.broadcasted_iota(i32, (HEAD_SIZE, 2 * HEAD_SIZE), 1)
    spread = (
        jnp.where(
            jnp.where(stat_row < 3, 0, jnp.where(stat_row < 6, 1, 2))
            == jnp.where(stat_col < HEAD_SIZE, 0, 1),
            1.0,
            0.0,
        )
        .astype(f32)
        .astype(bf16)
    )

    for load in loads[:6]:
        load.wait()
    scale = 1.0 / math.sqrt(HEAD_SIZE)
    count = per_group * G * slot_rows
    mask_shape = (per_group * G, slot_rows, own * suffix)
    block = lax.broadcasted_iota(i32, mask_shape, 0)
    if per_group > 1:
        block = lax.rem(block, G)
    row = lax.rem(lax.broadcasted_iota(i32, mask_shape, 1), own)
    column = lax.broadcasted_iota(i32, mask_shape, 2)
    bound = jnp.zeros(mask_shape, i32)
    for r in range(own):
        bound = jnp.where(row == r, r * suffix + len_ref[0, r], bound)
    bound = jnp.where(block == g, bound, 0).reshape(count, own * suffix)
    first = (row * suffix).reshape(count, own * suffix)
    column = column.reshape(count, own * suffix)
    in_suffix = (column >= first) & (column < bound)
    lane = lax.broadcasted_iota(i32, (count, HEAD_SIZE), 1)
    q32 = q_ref[0].astype(f32)
    for k in range(KEY_VALUE_HEADS):
        cut = slice(k * HEAD_SIZE, (k + 1) * HEAD_SIZE)
        stacked = jnp.concatenate(
            [
                q32[:, j * HEAD_SIZE : (j + 1) * HEAD_SIZE]
                for j in range(k * group, (k + 1) * group)
            ],
            0,
        ).astype(bf16)
        query = dot(to_slots, stacked).astype(bf16)
        scores = dot_nt(query, k_ref[0, :, cut]) * scale
        suf = dot_nt(query, sk_ref[0, :, :, cut].reshape(own * suffix, HEAD_SIZE)) * scale
        suf = jnp.where(in_suffix, suf, masked_score)
        peak = jnp.maximum(
            jnp.max(scores, -1, keepdims=True), jnp.max(suf, -1, keepdims=True)
        )
        terms = jnp.exp(scores - peak)
        suf_terms = jnp.where(in_suffix, jnp.exp(suf - peak), 0.0)
        mass = jnp.sum(terms, -1, keepdims=True) + jnp.sum(suf_terms, -1, keepdims=True)
        weighted = dot(terms.astype(bf16), v_ref[0, :, cut]) + dot(
            suf_terms.astype(bf16), sv_ref[0, :, :, cut].reshape(own * suffix, HEAD_SIZE)
        )
        value = jnp.where(lane < 3, peak, mass)
        top = value.astype(bf16).astype(f32)
        rest = value - top
        middle = rest.astype(bf16).astype(f32)
        low = rest - middle
        piece = jnp.where(
            (lane == 0) | (lane == 3), top, jnp.where((lane == 1) | (lane == 4), middle, low)
        )
        piece = jnp.where(lane < 6, piece, 0.0)
        message = jnp.concatenate(
            [
                weighted.reshape(per_group * G, slot_rows, HEAD_SIZE),
                piece.reshape(per_group * G, slot_rows, HEAD_SIZE),
            ],
            1,
        )
        s1[k * per_group * G : (k + 1) * per_group * G] = message.astype(bf16)

    pl.semaphore_wait(barrier, N - 1)

    def send_state(i, carry):
        d = lax.rem(me + i, N)
        pltpu.make_async_remote_copy(
            src_ref=s1.at[d],
            dst_ref=r1.at[me],
            send_sem=send_sem.at[0],
            recv_sem=recv_sem.at[0],
            device_id=(lax.rem(d, G), lax.div(d, G)),
            device_id_type=MESH,
        ).start()
        return carry

    lax.fori_loop(1, N, send_state, 0)
    r1[me] = s1[me]

    for load in loads[6:9]:
        load.wait()
    for c in range(chunks):
        cut = slice(c * chunk_width, (c + 1) * chunk_width)
        res_cr[c * own : (c + 1) * own, :] = res_ref[0, :, cut].astype(f32)
        gain_cr[c * own : (c + 1) * own, :] = jnp.broadcast_to(
            gain_ref[0:1, cut], (own, chunk_width)
        )
    loads[9].wait()

    def wait_all(ref, sem):
        pltpu.make_async_copy(ref, ref, sem).wait()

    wait_all(r1.at[pl.ds(0, N - 1)], recv_sem.at[0])

    states = r1[...].astype(f32)
    weighted = states[:, :slot_rows].reshape(H, G, slot_rows, HEAD_SIZE)
    pieces = states[:, slot_rows:].reshape(N * slot_rows, HEAD_SIZE).astype(bf16)
    stats = dot(pieces, spread)
    peaks = stats[:, :HEAD_SIZE].reshape(H, G, slot_rows, HEAD_SIZE)
    masses = stats[:, HEAD_SIZE:].reshape(H, G, slot_rows, HEAD_SIZE)
    best = jnp.max(peaks, 1)
    factors = jnp.exp(peaks - best[:, None])
    attention = jnp.sum(weighted * factors, 1) / jnp.sum(masses * factors, 1)
    attention = attention.reshape(H * slot_rows, HEAD_SIZE).astype(bf16)
    by_head = dot(to_heads, attention)
    attention = jnp.concatenate(
        [by_head[i * all_rows : (i + 1) * all_rows] for i in range(heads_dev)], 1
    ).astype(bf16)

    def deal(parts):
        return dot(to_owner, jnp.concatenate(parts, 0).astype(bf16)).astype(bf16)

    shares = deal(
        [
            dot(attention, ow_ref[:, c * chunk_width : (c + 1) * chunk_width])
            for c in range(chunks)
        ]
    )
    s2[...] = shares.reshape(H, 16, chunk_width)

    def to_peers(source, target, number):
        def send(i, carry):
            d = lax.rem(h + i, H)
            pltpu.make_async_remote_copy(
                src_ref=source(d),
                dst_ref=target,
                send_sem=send_sem.at[number],
                recv_sem=recv_sem.at[number],
                device_id=(g, d),
                device_id_type=MESH,
            ).start()
            return carry

        lax.fori_loop(1, H, send, 0)

    to_peers(lambda d: s2.at[d], r2.at[h], 1)
    r2[h] = s2[h]
    gain = gain_cr[...]
    hidden = res_cr[...]
    wait_all(r2.at[pl.ds(0, H - 1)], recv_sem.at[1])

    hidden = hidden + jnp.sum(r2[...].astype(f32), 0)
    row_sums = jnp.sum(hidden * hidden, 1, keepdims=True)
    row_of = lax.rem(lax.broadcasted_iota(i32, (16, 1), 0), own)
    total = jnp.zeros((16, 1), f32)
    for r in range(own):
        one = jnp.sum(jnp.where(row_of == r, row_sums, 0.0), 0, keepdims=True)
        total = jnp.where(row_of == r, one, total)
    normed = (hidden * lax.rsqrt(total / width + norm_epsilon) * gain).astype(bf16)
    s3[...] = normed
    to_peers(lambda d: s3, r3.at[h], 2)
    r3[h] = normed
    for load in loads[10:]:
        load.wait()
    wait_all(r3.at[pl.ds(0, H - 1)], recv_sem.at[2])

    arrived = dot(to_chunks, r3[...].reshape(H * 16, chunk_width))
    arrived = jnp.concatenate(
        [arrived[c * all_rows : (c + 1) * all_rows] for c in range(chunks)], 1
    ).astype(bf16)
    for e in range(local_experts):
        gate = dot(arrived, gw_ref[e])
        up = dot(arrived, uw_ref[e])
        act = (gate / (1.0 + jnp.exp(-gate)) * up).astype(bf16)
        made = deal(
            [
                dot(act, dw_ref[e, :, c * chunk_width : (c + 1) * chunk_width])
                for c in range(chunks)
            ]
        )
        s4[e] = made.reshape(H, 16, chunk_width)
        to_peers(lambda d: s4.at[e, d], r4.at[e, h], 3 + e)
        r4[e, h] = s4[e, h]

    logits = dot(arrived, rw_ref[...])
    row_at = lax.broadcasted_iota(i32, logits.shape, 0)
    wide_row = lax.rem(lax.broadcasted_iota(i32, (16, experts), 0), own)
    wide_expert = lax.broadcasted_iota(i32, (16, experts), 1)
    ids = ids_ref[0]
    own_logits = jnp.zeros((16, experts), f32)
    chosen = jnp.zeros((16, experts), f32)
    for r in range(own):
        line = jnp.sum(jnp.where(row_at == h * own + r, logits, 0.0), 0, keepdims=True)
        own_logits = jnp.where(wide_row == r, line, own_logits)
        for c in range(TOPK):
            hit = (wide_expert == ids[r : r + 1, c : c + 1]) & (wide_row == r)
            chosen = jnp.where(hit, 1.0, chosen)
    expo = jnp.where(chosen > 0.5, jnp.exp(own_logits), 0.0)
    route = expo / jnp.sum(expo, 1, keepdims=True)

    result = hidden
    for e in range(local_experts):
        wait_all(r4.at[e, pl.ds(0, H - 1)], recv_sem.at[3 + e])
        for p in range(H):
            name = p * local_experts + e
            result = result + route[:, name : name + 1] * r4[e, p].astype(f32)
    for c in range(chunks):
        out_ref[0, :, c * chunk_width : (c + 1) * chunk_width] = result[c * own : (c + 1) * own]

    wait_all(s1.at[pl.ds(0, N - 1)], send_sem.at[0])
    wait_all(s2.at[pl.ds(0, H - 1)], send_sem.at[1])
    wait_all(r3.at[pl.ds(0, H - 1)], send_sem.at[2])
    for e in range(local_experts):
        wait_all(s4.at[e, pl.ds(0, H - 1)], send_sem.at[3 + e])


def shards(*args):
    G = lax.axis_size("grp")
    H = lax.axis_size("head")
    args = list(args)
    residual, gain = args[6], args[8]
    args[8] = gain.reshape(1, -1)
    own, width = residual.shape[1], residual.shape[2]
    chunks = 16 // own
    chunk_width = width // chunks
    slot_rows = max(8, QUERY_HEADS // H * own)
    local_experts = args[10].shape[0]
    buffers = []
    for i, a in enumerate(args):
        if i == 5:
            buffers.append(pltpu.SMEM(a.shape, a.dtype))
        else:
            buffers.append(pltpu.VMEM(a.shape, a.dtype))
    N = G * H
    state = pltpu.VMEM((N, 2 * slot_rows, HEAD_SIZE), bf16)
    share = pltpu.VMEM((H, 16, chunk_width), bf16)
    made = pltpu.VMEM((local_experts, H, 16, chunk_width), bf16)
    return pl.pallas_call(
        functools.partial(kernel, G, H),
        out_shape=jax.ShapeDtypeStruct((1, own, width), f32),
        in_specs=[pl.BlockSpec(memory_space=pl.ANY)] * len(args),
        out_specs=pl.BlockSpec(memory_space=pltpu.VMEM),
        scratch_shapes=buffers
        + [
            state,
            state,
            share,
            share,
            pltpu.VMEM((16, chunk_width), bf16),
            share,
            made,
            made,
            pltpu.VMEM((16, chunk_width), f32),
            pltpu.VMEM((16, chunk_width), f32),
            pltpu.SemaphoreType.DMA((len(args),)),
            pltpu.SemaphoreType.DMA((3 + local_experts,)),
            pltpu.SemaphoreType.DMA((3 + local_experts,)),
        ],
        compiler_params=pltpu.CompilerParams(
            collective_id=0, has_side_effects=True, vmem_limit_bytes=56 * 1024 * 1024
        ),
        name="decode_layer",
    )(*args)


def solution(mesh):
    return jax.shard_map(
        shards,
        mesh=mesh,
        in_specs=(
            P("head", None, None),
            P("head", "grp", None),
            P("head", "grp", None),
            P("head", "grp", None, None),
            P("head", "grp", None, None),
            P("head", "grp"),
            P("head", "grp", None),
            P("head", None),
            P(),
            P(),
            P("head", None, None),
            P("head", None, None),
            P("head", None, None),
            P("head", "grp", None),
        ),
        out_specs=P("head", "grp", None),
        check_vma=False,
    )
```

time: 166 us -> 28.9 us (0.17)
  waiting for transfers between devices: 83.8 us -> 0 us
  starting transfers between devices: 30.1 us -> 0 us
  Pallas kernels: 0 us -> 25.5 us
  between operations: 14.3 us -> 0.01 us
  local copies, waits for them, and re-layouts: 15.3 us -> 3.16 us
  matrix products: 11.5 us -> 0 us
  other arithmetic: 10 us -> 0 us
    unnamed x2 -> x0, waiting for transfers between devices: 50.5 us -> none
    all_to_all x8 -> x0, waiting for transfers between devices: 33.4 us -> none  [the longest x1 5.53 us: shards(): lax.all_to_all(weighted_parts, 'grp', split_axis=1, concat_axis=1, tiled=...]
    all_to_all x8 -> x0, starting transfers between devices: 30 us -> none  [the longest x1 6.32 us: shards(): lax.all_to_all(peak_parts, 'grp', split_axis=1, concat_axis=1, tiled=True)]
    pallas_call x0 -> x1, Pallas kernels: none -> 25.5 us  [shards(): pl.pallas_call(functools.partial(kernel, G, H), out_shape=jax.ShapeDtypeS...]
    dot_general x9 -> x0, matrix products: 11.5 us -> none  [the longest x1 2.83 us: shards(): jnp.einsum('secf,efd->secd', inner_act, down_weights, preferred_element_t...]
    another operation x6 -> x0, local copies, waits for them, and re-layouts: 5.39 us -> none  [the longest x1 1.37 us: shards(): row_suffix_keys[0].reshape(prompt_own_rows, -1, KEY_VALUE_HEADS, HEAD_SIZE)]
    reduce_sum x9 -> x0, other arithmetic: 3.29 us -> none  [the longest x1 0.97 us: shards(): mean_square = jnp.mean(hidden_state * hidden_state, -1, keepdims=True)]
    all_to_all x6 -> x0, local copies, waits for them, and re-layouts: 2.62 us -> none  [the longest x1 0.74 us: shards(): lax.all_to_all(weighted_parts, 'grp', split_axis=1, concat_axis=1, tiled=...]
  transfers between devices with their start and end apart: 9 -> 0, of which waited for: 9 -> 0; matrix products, arithmetic and copies ran while one was open for 5% -> 0% of each run, Pallas kernels for 0% -> 0%
where the time goes in v1:
time: 28.9 us; the launch traced here: 28.7 us
  Pallas kernels  25.5 us (88%)
  local copies, waits for them, and re-layouts  3.16 us (11%)
    pallas_call x1, Pallas kernels, shards(): pl.pallas_call(functools.partial(kernel, G, H), out_shape=jax.ShapeDtypeS...  25.5 us
    unnamed x2, local copies, waits for them, and re-layouts  3.16 us

profile of v1, /device:TPU:0, one launch (start us, length us, event | category | flops | bytes accessed | tf_op | source)
XLA Modules:
  0.0 28.7 jit_solution(9528125962647737957)
XLA Ops:
  0.0 1.8 %copy.15.rw_hbm = bf16[2048,16]{1,0:T(8,128)(2,1)} copy(bf16[2048,16]{0,1:T(8,128)(2,1)} %param.23) | data formatting | bytes 131072 | tf_op args[9]
  1.8 25.5 %decode_layer.1 = f32[1,2,2048]{2,1,0:T(2,128)} custom-call(bf16[1,8,4096]{2,1,0:T(8,128)(2,1)} %q_hbm.1, bf16[1,128,512]{2,1,0:T(8,128)(2,1)} %k_hbm.1, bf16[1,128,512]{2,1,0:T(8,128)(2,1)} %v_hbm.1, bf16[1,2,16,512]{3,2,1,0:T(8,128)(2,1)} %sk_hbm.1, bf16[1,2,16,512]{3,2,1,0:T(8,128)(2,1)} %sv_hbm.1, s32[1,2]{1,0:T(1,128)} %len_hbm.1, ...), custom_call_target="tpu_custom_call" | custom-call | tf_op jit(solution)/shard_map/decode_layer/pallas_call | solution.py:392
  27.3 1.3 %copy.17 = f32[1,2,2048]{2,1,0:T(2,128)} copy(f32[1,2,2048]{2,1,0:T(2,128)} %decode_layer.1) | data formatting | bytes 32768

commit v2 on v1

v2 whole, which is shorter than its diff:
```python
import functools
import math

import jax
import jax.numpy as jnp
from jax import lax
from jax.experimental import pallas as pl
from jax.experimental.pallas import tpu as pltpu
from jax.sharding import PartitionSpec as P

QUERY_HEADS = 32
KEY_VALUE_HEADS = 4
HEAD_SIZE = 128
TOPK = 8

masked_score = -1e30
norm_epsilon = 1e-06
f32, bf16, i32 = jnp.float32, jnp.bfloat16, jnp.int32
MESH = pl.DeviceIdType.MESH


def dot(a, b):
    return jnp.dot(a, b, preferred_element_type=f32)


def dot_nt(a, b):
    return lax.dot_general(a, b, (((1,), (1,)), ((), ())), preferred_element_type=f32)


def one_hot(shape, source):
    a = lax.broadcasted_iota(i32, shape, 0)
    b = lax.broadcasted_iota(i32, shape, 1)
    col = lax.broadcasted_iota(i32, shape, 2)
    hit = jnp.where(source(a, b) == col, 1.0, 0.0).astype(f32)
    return hit.reshape(shape[0] * shape[1], shape[2]).astype(bf16)


def kernel(
    G,
    H,
    q_hbm,
    k_hbm,
    v_hbm,
    sk_hbm,
    sv_hbm,
    len_hbm,
    res_hbm,
    ow_hbm,
    gain_hbm,
    rw_hbm,
    gw_hbm,
    uw_hbm,
    dw_hbm,
    ids_hbm,
    out_ref,
    q_ref,
    k_ref,
    v_ref,
    sk_ref,
    sv_ref,
    len_ref,
    res_ref,
    ow_ref,
    gain_ref,
    rw_ref,
    gw_ref,
    uw_ref,
    dw_ref,
    ids_ref,
    s1,
    r1,
    s2,
    r2,
    s3,
    r3,
    s4,
    r4,
    s5,
    r5,
    gain_cr,
    res_cr,
    load_sem,
    send_sem,
    recv_sem,
):
    g = lax.axis_index("grp")
    h = lax.axis_index("head")

    rows = q_ref.shape[1]
    own = res_ref.shape[1]
    width = res_ref.shape[2]
    suffix = sk_ref.shape[2]
    group = QUERY_HEADS // KEY_VALUE_HEADS
    heads_dev = QUERY_HEADS // H
    per_group = group // heads_dev
    slot_rows = s5.shape[1] // 2
    chunks, chunk_width = 16 // own, s2.shape[2]
    all_rows = H * own
    local_experts = gw_ref.shape[0]


    pairs = [
        (q_hbm, q_ref),
        (k_hbm, k_ref),
        (len_hbm, len_ref),
        (sk_hbm, sk_ref),
        (v_hbm, v_ref),
        (sv_hbm, sv_ref),
        (res_hbm, res_ref),
        (gain_hbm, gain_ref),
        (ids_hbm, ids_ref),
        (ow_hbm, ow_ref),
        (rw_hbm, rw_ref),
        (gw_hbm, gw_ref),
        (uw_hbm, uw_ref),
        (dw_hbm, dw_ref),
    ]
    loads = [pltpu.make_async_copy(a, b, load_sem.at[i]) for i, (a, b) in enumerate(pairs)]
    for load in loads:
        load.start()

    def other_group(i):
        return (lax.rem(g + i, G), h)

    def other_head(i):
        return (g, lax.rem(h + i, H))

    barrier = pltpu.get_barrier_semaphore()
    for i in range(1, G):
        pl.semaphore_signal(barrier, inc=1, device_id=other_group(i), device_id_type=MESH)
    for i in range(1, H):
        pl.semaphore_signal(barrier, inc=1, device_id=other_head(i), device_id_type=MESH)

    def query_source(a, b):
        block, head_block = lax.div(a, per_group), lax.rem(a, per_group)
        head, row = lax.div(b, own), lax.rem(b, own)
        found = (head_block * heads_dev + head) * rows + block * own + row
        return jnp.where(b < heads_dev * own, found, -1)

    def head_source(a, b):
        offset = jnp.where(a < heads_dev, a * own, slot_rows)
        return lax.div(b, own) * 2 * slot_rows + offset + lax.rem(b, own)

    to_slots = one_hot((G * per_group, slot_rows, group * rows), query_source)
    to_heads = one_hot((heads_dev + 1, all_rows, H * 2 * slot_rows), head_source)
    to_owner = one_hot(
        (H, 16, chunks * all_rows),
        lambda a, b: lax.div(b, own) * all_rows + a * own + lax.rem(b, own),
    )
    to_chunks = one_hot(
        (chunks, all_rows, H * 16),
        lambda a, b: lax.div(b, own) * 16 + a * own + lax.rem(b, own),
    )

    for load in loads[:6]:
        load.wait()
    scale = 1.0 / math.sqrt(HEAD_SIZE)
    part = per_group * slot_rows
    count = G * part
    mask_shape = (G * per_group, slot_rows, own * suffix)
    block = lax.div(lax.broadcasted_iota(i32, mask_shape, 0), per_group)
    row = lax.rem(lax.broadcasted_iota(i32, mask_shape, 1), own)
    column = lax.broadcasted_iota(i32, mask_shape, 2)
    bound = jnp.zeros(mask_shape, i32)
    for r in range(own):
        bound = jnp.where(row == r, r * suffix + len_ref[0, r], bound)
    bound = jnp.where(block == g, bound, 0).reshape(count, own * suffix)
    first = (row * suffix).reshape(count, own * suffix)
    column = column.reshape(count, own * suffix)
    in_suffix = (column >= first) & (column < bound)
    lane = lax.broadcasted_iota(i32, (count, HEAD_SIZE), 1)
    pieces = jnp.zeros((count, HEAD_SIZE), f32)
    q32 = q_ref[0].astype(f32)
    for k in range(KEY_VALUE_HEADS):
        cut = slice(k * HEAD_SIZE, (k + 1) * HEAD_SIZE)
        stacked = jnp.concatenate(
            [
                q32[:, j * HEAD_SIZE : (j + 1) * HEAD_SIZE]
                for j in range(k * group, (k + 1) * group)
            ],
            0,
        ).astype(bf16)
        query = dot(to_slots, stacked).astype(bf16)
        scores = dot_nt(query, k_ref[0, :, cut]) * scale
        suf = dot_nt(query, sk_ref[0, :, :, cut].reshape(own * suffix, HEAD_SIZE)) * scale
        suf = jnp.where(in_suffix, suf, masked_score)
        peak = jnp.maximum(
            jnp.max(scores, -1, keepdims=True), jnp.max(suf, -1, keepdims=True)
        )
        terms = jnp.exp(scores - peak)
        suf_terms = jnp.where(in_suffix, jnp.exp(suf - peak), 0.0)
        mass = jnp.sum(terms, -1, keepdims=True) + jnp.sum(suf_terms, -1, keepdims=True)
        weighted = dot(terms.astype(bf16), v_ref[0, :, cut]) + dot(
            suf_terms.astype(bf16), sv_ref[0, :, :, cut].reshape(own * suffix, HEAD_SIZE)
        )
        s1[:, k * part : (k + 1) * part, :] = weighted.reshape(G, part, HEAD_SIZE).astype(bf16)
        at = lane - 8 * k
        value = jnp.where(at < 3, peak, mass)
        top = value.astype(bf16).astype(f32)
        rest = value - top
        middle = rest.astype(bf16).astype(f32)
        low = rest - middle
        piece = jnp.where(
            (at == 0) | (at == 3), top, jnp.where((at == 1) | (at == 4), middle, low)
        )
        pieces = jnp.where((at >= 0) & (at < 6), piece, pieces)
    s1[:, KEY_VALUE_HEADS * part :, :] = pieces.reshape(G, part, HEAD_SIZE).astype(bf16)

    pl.semaphore_wait(barrier, G + H - 2)

    for i in range(1, G):
        to = other_group(i)
        pltpu.make_async_remote_copy(
            src_ref=s1.at[to[0]],
            dst_ref=r1.at[g],
            send_sem=send_sem.at[0],
            recv_sem=recv_sem.at[0],
            device_id=to,
            device_id_type=MESH,
        ).start()
    r1[g] = s1[g]

    for load in loads[6:9]:
        load.wait()
    for c in range(chunks):
        cut = slice(c * chunk_width, (c + 1) * chunk_width)
        res_cr[c * own : (c + 1) * own, :] = res_ref[0, :, cut].astype(f32)
        gain_cr[c * own : (c + 1) * own, :] = jnp.broadcast_to(
            gain_ref[0:1, cut], (own, chunk_width)
        )
    ids = ids_ref[0].astype(f32)
    id_row = lax.rem(lax.broadcasted_iota(i32, (slot_rows, HEAD_SIZE), 0), own)
    id_lane = lax.broadcasted_iota(i32, (slot_rows, HEAD_SIZE), 1)
    id_tile = jnp.zeros((slot_rows, HEAD_SIZE), f32)
    for r in range(own):
        for c in range(TOPK):
            id_tile = jnp.where(
                (id_row == r) & (id_lane == c), ids[r : r + 1, c : c + 1], id_tile
            )
    id_tile = jnp.broadcast_to(id_tile[None], (per_group, slot_rows, HEAD_SIZE))
    stat_row = lax.broadcasted_iota(i32, (HEAD_SIZE, 2 * HEAD_SIZE), 0)
    stat_col = lax.broadcasted_iota(i32, (HEAD_SIZE, 2 * HEAD_SIZE), 1)
    stat_low = jnp.where(stat_col < HEAD_SIZE, 0, 3)

    def wait_all(ref, sem):
        pltpu.make_async_copy(ref, ref, sem).wait()

    def to_peers(source, target, number):
        for i in range(1, H):
            to = other_head(i)
            pltpu.make_async_remote_copy(
                src_ref=source(to[1]),
                dst_ref=target,
                send_sem=send_sem.at[number],
                recv_sem=recv_sem.at[number],
                device_id=to,
                device_id_type=MESH,
            ).start()

    wait_all(r1.at[pl.ds(0, G - 1)], recv_sem.at[0])

    got = r1[:, KEY_VALUE_HEADS * part :, :].reshape(count, HEAD_SIZE)
    for k in range(KEY_VALUE_HEADS):
        low = stat_low + 8 * k
        spread = jnp.where((stat_row >= low) & (stat_row < low + 3), 1.0, 0.0).astype(f32)
        stats = dot(got, spread.astype(bf16))
        peaks = stats[:, :HEAD_SIZE].reshape(G, part, HEAD_SIZE)
        masses = stats[:, HEAD_SIZE:].reshape(G, part, HEAD_SIZE)
        weighted = r1[:, k * part : (k + 1) * part, :].astype(f32)
        factors = jnp.exp(peaks - jnp.max(peaks, 0)[None])
        mine = jnp.sum(weighted * factors, 0) / jnp.sum(masses * factors, 0)
        message = jnp.concatenate([mine.reshape(per_group, slot_rows, HEAD_SIZE), id_tile], 1)
        s5[k * per_group : (k + 1) * per_group] = message.astype(bf16)
    to_peers(lambda d: s5.at[d], r5.at[h], 4)
    r5[h] = s5[h]
    loads[9].wait()
    wait_all(r5.at[pl.ds(0, H - 1)], recv_sem.at[4])
    by_head = dot(to_heads, r5[...].reshape(H * 2 * slot_rows, HEAD_SIZE))
    attention = jnp.concatenate(
        [by_head[i * all_rows : (i + 1) * all_rows] for i in range(heads_dev)], 1
    ).astype(bf16)
    all_ids = by_head[heads_dev * all_rows :]

    def deal(parts):
        return dot(to_owner, jnp.concatenate(parts, 0).astype(bf16)).astype(bf16)

    shares = deal(
        [
            dot(attention, ow_ref[:, c * chunk_width : (c + 1) * chunk_width])
            for c in range(chunks)
        ]
    )
    s2[...] = shares.reshape(H, 16, chunk_width)

    to_peers(lambda d: s2.at[d], r2.at[h], 1)
    r2[h] = s2[h]
    gain = gain_cr[...]
    hidden = res_cr[...]
    wait_all(r2.at[pl.ds(0, H - 1)], recv_sem.at[1])

    hidden = hidden + jnp.sum(r2[...].astype(f32), 0)
    row_sums = jnp.sum(hidden * hidden, 1, keepdims=True)
    row_of = lax.rem(lax.broadcasted_iota(i32, (16, 1), 0), own)
    total = jnp.zeros((16, 1), f32)
    for r in range(own):
        one = jnp.sum(jnp.where(row_of == r, row_sums, 0.0), 0, keepdims=True)
        total = jnp.where(row_of == r, one, total)
    normed = (hidden * lax.rsqrt(total / width + norm_epsilon) * gain).astype(bf16)
    s3[...] = normed
    to_peers(lambda d: s3, r3.at[h], 2)
    r3[h] = normed
    for load in loads[10:]:
        load.wait()
    wait_all(r3.at[pl.ds(0, H - 1)], recv_sem.at[2])

    arrived = dot(to_chunks, r3[...].reshape(H * 16, chunk_width))
    arrived = jnp.concatenate(
        [arrived[c * all_rows : (c + 1) * all_rows] for c in range(chunks)], 1
    ).astype(bf16)
    logits = dot_nt(arrived, rw_ref[...])
    expert_at = lax.broadcasted_iota(i32, logits.shape, 1)
    expert_at_float = expert_at.astype(f32)
    chosen = jnp.zeros(logits.shape, f32)
    for c in range(TOPK):
        chosen = jnp.where(expert_at_float == all_ids[:, c : c + 1], 1.0, chosen)
    expo = jnp.where(chosen > 0.5, jnp.exp(logits), 0.0)
    route = expo / jnp.sum(expo, 1, keepdims=True)

    mixed = [jnp.zeros((all_rows, chunk_width), f32)] * chunks
    for e in range(local_experts):
        gate = dot(arrived, gw_ref[e])
        up = dot(arrived, uw_ref[e])
        act = (gate / (1.0 + jnp.exp(-gate)) * up).astype(bf16)
        name = h * local_experts + e
        share = jnp.sum(jnp.where(expert_at == name, route, 0.0), 1, keepdims=True)
        for c in range(chunks):
            made = dot(act, dw_ref[e, :, c * chunk_width : (c + 1) * chunk_width])
            mixed[c] = mixed[c] + share * made.astype(bf16).astype(f32)
    s4[...] = deal(mixed).reshape(H, 16, chunk_width)
    to_peers(lambda d: s4.at[d], r4.at[h], 3)
    r4[h] = s4[h]
    wait_all(r4.at[pl.ds(0, H - 1)], recv_sem.at[3])
    result = hidden + jnp.sum(r4[...].astype(f32), 0)
    for c in range(chunks):
        out_ref[0, :, c * chunk_width : (c + 1) * chunk_width] = result[c * own : (c + 1) * own]

    wait_all(s1.at[pl.ds(0, G - 1)], send_sem.at[0])
    wait_all(s5.at[pl.ds(0, H - 1)], send_sem.at[4])
    wait_all(s2.at[pl.ds(0, H - 1)], send_sem.at[1])
    wait_all(r3.at[pl.ds(0, H - 1)], send_sem.at[2])
    wait_all(s4.at[pl.ds(0, H - 1)], send_sem.at[3])


def shards(*args):
    G = lax.axis_size("grp")
    H = lax.axis_size("head")
    args = list(args)
    residual, gain = args[6], args[8]
    args[8] = gain.reshape(1, -1)
    args[9] = args[9].T
    own, width = residual.shape[1], residual.shape[2]
    chunks = 16 // own
    chunk_width = width // chunks
    slot_rows = max(8, QUERY_HEADS // H * own)
    buffers = []
    for i, a in enumerate(args):
        if i == 5:
            buffers.append(pltpu.SMEM(a.shape, a.dtype))
        else:
            buffers.append(pltpu.VMEM(a.shape, a.dtype))
    per_group = QUERY_HEADS // KEY_VALUE_HEADS * H // QUERY_HEADS
    state_rows = (KEY_VALUE_HEADS + 1) * per_group * slot_rows
    state = pltpu.VMEM((G, state_rows, HEAD_SIZE), bf16)
    share = pltpu.VMEM((H, 16, chunk_width), bf16)
    slot = pltpu.VMEM((H, 2 * slot_rows, HEAD_SIZE), bf16)
    return pl.pallas_call(
        functools.partial(kernel, G, H),
        out_shape=jax.ShapeDtypeStruct((1, own, width), f32),
        in_specs=[pl.BlockSpec(memory_space=pl.ANY)] * len(args),
        out_specs=pl.BlockSpec(memory_space=pltpu.VMEM),
        scratch_shapes=buffers
        + [
            state,
            state,
            share,
            share,
            pltpu.VMEM((16, chunk_width), bf16),
            share,
            share,
            share,
            slot,
            slot,
            pltpu.VMEM((16, chunk_width), f32),
            pltpu.VMEM((16, chunk_width), f32),
            pltpu.SemaphoreType.DMA((len(args),)),
            pltpu.SemaphoreType.DMA((5,)),
            pltpu.SemaphoreType.DMA((5,)),
        ],
        compiler_params=pltpu.CompilerParams(
            collective_id=0, has_side_effects=True, vmem_limit_bytes=56 * 1024 * 1024
        ),
        name="decode_layer",
    )(*args)


def solution(mesh):
    return jax.shard_map(
        shards,
        mesh=mesh,
        in_specs=(
            P("head", None, None),
            P("head", "grp", None),
            P("head", "grp", None),
            P("head", "grp", None, None),
            P("head", "grp", None, None),
            P("head", "grp"),
            P("head", "grp", None),
            P("head", None),
            P(),
            P(),
            P("head", None, None),
            P("head", None, None),
            P("head", None, None),
            P("head", "grp", None),
        ),
        out_specs=P("head", "grp", None),
        check_vma=False,
    )
```

time: 28.9 us -> 27.2 us (0.941)
  local copies, waits for them, and re-layouts: 3.16 us -> 1.32 us
    unnamed x2 -> x1, local copies, waits for them, and re-layouts: 3.16 us -> 1.32 us
where the time goes in v2:
time: 27.2 us; the launch traced here: 26.9 us
  Pallas kernels  25.6 us (94%)
  local copies, waits for them, and re-layouts  1.32 us (5%)
    pallas_call x1, Pallas kernels, shards(): pl.pallas_call(functools.partial(kernel, G, H), out_shape=jax.ShapeDtypeS...  25.6 us
    unnamed x1, local copies, waits for them, and re-layouts  1.32 us

profile of v2, /device:TPU:0, one launch (start us, length us, event | category | flops | bytes accessed | tf_op | source)
XLA Modules:
  0.0 26.9 jit_solution(7048201134992021870)
XLA Ops:
  0.0 25.6 %decode_layer.1 = f32[1,2,2048]{2,1,0:T(2,128)} custom-call(bf16[1,8,4096]{2,1,0:T(8,128)(2,1)} %q_hbm.1, bf16[1,128,512]{2,1,0:T(8,128)(2,1)} %k_hbm.1, bf16[1,128,512]{2,1,0:T(8,128)(2,1)} %v_hbm.1, bf16[1,2,16,512]{3,2,1,0:T(8,128)(2,1)} %sk_hbm.1, bf16[1,2,16,512]{3,2,1,0:T(8,128)(2,1)} %sv_hbm.1, s32[1,2]{1,0:T(1,128)} %len_hbm.1, ...), custom_call_target="tpu_custom_call" | custom-call | tf_op jit(solution)/shard_map/decode_layer/pallas_call | solution.py:376
  25.6 1.3 %copy.16 = f32[1,2,2048]{2,1,0:T(2,128)} copy(f32[1,2,2048]{2,1,0:T(2,128)} %decode_layer.1) | data formatting | bytes 32768

commit v3 on v2

--- a/solution.py
+++ b/solution.py
@@ -25,6 +25,14 @@
 
 def dot_nt(a, b):
     return lax.dot_general(a, b, (((1,), (1,)), ((), ())), preferred_element_type=f32)
+
+
+def div(a, n):
+    return a >> (n.bit_length() - 1) if n & (n - 1) == 0 else lax.div(a, n)
+
+
+def rem(a, n):
+    return a & (n - 1) if n & (n - 1) == 0 else lax.rem(a, n)
 
 
 def one_hot(shape, source):
@@ -52,7 +60,8 @@
     uw_hbm,
     dw_hbm,
     ids_hbm,
-    out_ref,
+    hidden_ref,
+    routed_ref,
     q_ref,
     k_ref,
     v_ref,
@@ -63,8 +72,7 @@
     ow_ref,
     gain_ref,
     rw_ref,
-    gw_ref,
-    uw_ref,
+    gu_ref,
     dw_ref,
     ids_ref,
     s1,
@@ -96,7 +104,6 @@
     slot_rows = s5.shape[1] // 2
     chunks, chunk_width = 16 // own, s2.shape[2]
     all_rows = H * own
-    local_experts = gw_ref.shape[0]
 
 
     pairs = [
@@ -111,10 +118,13 @@
         (ids_hbm, ids_ref),
         (ow_hbm, ow_ref),
         (rw_hbm, rw_ref),
-        (gw_hbm, gw_ref),
-        (uw_hbm, uw_ref),
-        (dw_hbm, dw_ref),
     ]
+    local_experts, _, hidden_units = gw_hbm.shape
+    for e in range(local_experts):
+        for j, source in enumerate((gw_hbm, uw_hbm)):
+            columns = pl.ds((2 * e + j) * hidden_units, hidden_units)
+            pairs.append((source.at[e], gu_ref.at[:, columns]))
+        pairs.append((dw_hbm.at[e], dw_ref.at[pl.ds(e * hidden_units, hidden_units)]))
     loads = [pltpu.make_async_copy(a, b, load_sem.at[i]) for i, (a, b) in enumerate(pairs)]
     for load in loads:
         load.start()
@@ -132,24 +142,24 @@
         pl.semaphore_signal(barrier, inc=1, device_id=other_head(i), device_id_type=MESH)
 
     def query_source(a, b):
-        block, head_block = lax.div(a, per_group), lax.rem(a, per_group)
-        head, row = lax.div(b, own), lax.rem(b, own)
+        block, head_block = div(a, per_group), rem(a, per_group)
+        head, row = div(b, own), rem(b, own)
         found = (head_block * heads_dev + head) * rows + block * own + row
         return jnp.where(b < heads_dev * own, found, -1)
 
     def head_source(a, b):
         offset = jnp.where(a < heads_dev, a * own, slot_rows)
-        return lax.div(b, own) * 2 * slot_rows + offset + lax.rem(b, own)
+        return div(b, own) * 2 * slot_rows + offset + rem(b, own)
 
     to_slots = one_hot((G * per_group, slot_rows, group * rows), query_source)
     to_heads = one_hot((heads_dev + 1, all_rows, H * 2 * slot_rows), head_source)
     to_owner = one_hot(
         (H, 16, chunks * all_rows),
-        lambda a, b: lax.div(b, own) * all_rows + a * own + lax.rem(b, own),
+        lambda a, b: div(b, own) * all_rows + a * own + rem(b, own),
     )
     to_chunks = one_hot(
         (chunks, all_rows, H * 16),
-        lambda a, b: lax.div(b, own) * 16 + a * own + lax.rem(b, own),
+        lambda a, b: div(b, own) * 16 + a * own + rem(b, own),
     )
 
     for load in loads[:6]:
@@ -157,19 +167,23 @@
     scale = 1.0 / math.sqrt(HEAD_SIZE)
     part = per_group * slot_rows
     count = G * part
-    mask_shape = (G * per_group, slot_rows, own * suffix)
-    block = lax.div(lax.broadcasted_iota(i32, mask_shape, 0), per_group)
-    row = lax.rem(lax.broadcasted_iota(i32, mask_shape, 1), own)
+    prefix = k_ref.shape[1]
+    pad = -(own * suffix) % HEAD_SIZE
+    padded = own * suffix + pad
+    mask_shape = (G * per_group, slot_rows, padded)
+    block = div(lax.broadcasted_iota(i32, mask_shape, 0), per_group)
+    row = rem(lax.broadcasted_iota(i32, mask_shape, 1), own)
     column = lax.broadcasted_iota(i32, mask_shape, 2)
     bound = jnp.zeros(mask_shape, i32)
     for r in range(own):
         bound = jnp.where(row == r, r * suffix + len_ref[0, r], bound)
-    bound = jnp.where(block == g, bound, 0).reshape(count, own * suffix)
-    first = (row * suffix).reshape(count, own * suffix)
-    column = column.reshape(count, own * suffix)
+    bound = jnp.where(block == g, bound, 0).reshape(count, padded)
+    first = (row * suffix).reshape(count, padded)
+    column = column.reshape(count, padded)
     in_suffix = (column >= first) & (column < bound)
     lane = lax.broadcasted_iota(i32, (count, HEAD_SIZE), 1)
     pieces = jnp.zeros((count, HEAD_SIZE), f32)
+    blank = jnp.zeros((pad, HEAD_SIZE), bf16)
     q32 = q_ref[0].astype(f32)
     for k in range(KEY_VALUE_HEADS):
         cut = slice(k * HEAD_SIZE, (k + 1) * HEAD_SIZE)
@@ -181,18 +195,19 @@
             0,
         ).astype(bf16)
         query = dot(to_slots, stacked).astype(bf16)
-        scores = dot_nt(query, k_ref[0, :, cut]) * scale
-        suf = dot_nt(query, sk_ref[0, :, :, cut].reshape(own * suffix, HEAD_SIZE)) * scale
-        suf = jnp.where(in_suffix, suf, masked_score)
-        peak = jnp.maximum(
-            jnp.max(scores, -1, keepdims=True), jnp.max(suf, -1, keepdims=True)
-        )
+        keys = sk_ref[0, :, :, cut].reshape(own * suffix, HEAD_SIZE)
+        keys = jnp.concatenate([k_ref[0, :, cut], keys, blank], 0)
+        values = sv_ref[0, :, :, cut].reshape(own * suffix, HEAD_SIZE)
+        values = jnp.concatenate([v_ref[0, :, cut], values, blank], 0)
+        scores = dot_nt(query, keys) * scale
+        suf = jnp.where(in_suffix, scores[:, prefix:], masked_score)
+        scores = jnp.concatenate([scores[:, :prefix], suf], 1)
+        peak = jnp.max(scores, -1, keepdims=True)
         terms = jnp.exp(scores - peak)
-        suf_terms = jnp.where(in_suffix, jnp.exp(suf - peak), 0.0)
-        mass = jnp.sum(terms, -1, keepdims=True) + jnp.sum(suf_terms, -1, keepdims=True)
-        weighted = dot(terms.astype(bf16), v_ref[0, :, cut]) + dot(
-            suf_terms.astype(bf16), sv_ref[0, :, :, cut].reshape(own * suffix, HEAD_SIZE)
-        )
+        suf = jnp.where(in_suffix, terms[:, prefix:], 0.0)
+        terms = jnp.concatenate([terms[:, :prefix], suf], 1)
+        mass = jnp.sum(terms, -1, keepdims=True)
+        weighted = dot(terms.astype(bf16), values)
         s1[:, k * part : (k + 1) * part, :] = weighted.reshape(G, part, HEAD_SIZE).astype(bf16)
         at = lane - 8 * k
         value = jnp.where(at < 3, peak, mass)
@@ -309,6 +324,9 @@
     s3[...] = normed
     to_peers(lambda d: s3, r3.at[h], 2)
     r3[h] = normed
+    for c in range(chunks):
+        cut = slice(c * chunk_width, (c + 1) * chunk_width)
+        hidden_ref[0, :, cut] = hidden[c * own : (c + 1) * own]
     for load in loads[10:]:
         load.wait()
     wait_all(r3.at[pl.ds(0, H - 1)], recv_sem.at[2])
@@ -326,23 +344,25 @@
     expo = jnp.where(chosen > 0.5, jnp.exp(logits), 0.0)
     route = expo / jnp.sum(expo, 1, keepdims=True)
 
-    mixed = [jnp.zeros((all_rows, chunk_width), f32)] * chunks
+    inner = dot(arrived, gu_ref[...])
+    acts = []
     for e in range(local_experts):
-        gate = dot(arrived, gw_ref[e])
-        up = dot(arrived, uw_ref[e])
-        act = (gate / (1.0 + jnp.exp(-gate)) * up).astype(bf16)
+        gate = inner[:, 2 * e * hidden_units : (2 * e + 1) * hidden_units]
+        up = inner[:, (2 * e + 1) * hidden_units : (2 * e + 2) * hidden_units]
         name = h * local_experts + e
         share = jnp.sum(jnp.where(expert_at == name, route, 0.0), 1, keepdims=True)
-        for c in range(chunks):
-            made = dot(act, dw_ref[e, :, c * chunk_width : (c + 1) * chunk_width])
-            mixed[c] = mixed[c] + share * made.astype(bf16).astype(f32)
+        acts.append((gate / (1.0 + jnp.exp(-gate)) * up * share).astype(bf16))
+    acts = jnp.concatenate(acts, 1)
+    mixed = [
+        dot(acts, dw_ref[:, c * chunk_width : (c + 1) * chunk_width]) for c in range(chunks)
+    ]
     s4[...] = deal(mixed).reshape(H, 16, chunk_width)
     to_peers(lambda d: s4.at[d], r4.at[h], 3)
     r4[h] = s4[h]
     wait_all(r4.at[pl.ds(0, H - 1)], recv_sem.at[3])
-    result = hidden + jnp.sum(r4[...].astype(f32), 0)
+    result = jnp.sum(r4[...].astype(f32), 0)
     for c in range(chunks):
-        out_ref[0, :, c * chunk_width : (c + 1) * chunk_width] = result[c * own : (c + 1) * own]
+        routed_ref[0, :, c * chunk_width : (c + 1) * chunk_width] = result[c * own : (c + 1) * own]
 
     wait_all(s1.at[pl.ds(0, G - 1)], send_sem.at[0])
     wait_all(s5.at[pl.ds(0, H - 1)], send_sem.at[4])
@@ -363,8 +383,15 @@
     chunk_width = width // chunks
     slot_rows = max(8, QUERY_HEADS // H * own)
     buffers = []
+    local_experts, depth, hidden_units = args[10].shape
     for i, a in enumerate(args):
-        if i == 5:
+        if i == 10:
+            buffers.append(pltpu.VMEM((depth, 2 * local_experts * hidden_units), a.dtype))
+        elif i == 11:
+            continue
+        elif i == 12:
+            buffers.append(pltpu.VMEM((local_experts * hidden_units, width), a.dtype))
+        elif i == 5:
             buffers.append(pltpu.SMEM(a.shape, a.dtype))
         else:
             buffers.append(pltpu.VMEM(a.shape, a.dtype))
@@ -373,11 +400,12 @@
     state = pltpu.VMEM((G, state_rows, HEAD_SIZE), bf16)
     share = pltpu.VMEM((H, 16, chunk_width), bf16)
     slot = pltpu.VMEM((H, 2 * slot_rows, HEAD_SIZE), bf16)
-    return pl.pallas_call(
+    part = pltpu.VMEM((1, own, width), f32)
+    hidden, routed = pl.pallas_call(
         functools.partial(kernel, G, H),
-        out_shape=jax.ShapeDtypeStruct((1, own, width), f32),
+        out_shape=(part, part),
         in_specs=[pl.BlockSpec(memory_space=pl.ANY)] * len(args),
-        out_specs=pl.BlockSpec(memory_space=pltpu.VMEM),
+        out_specs=[pl.BlockSpec(memory_space=pltpu.VMEM)] * 2,
         scratch_shapes=buffers
         + [
             state,
@@ -392,7 +420,7 @@
             slot,
             pltpu.VMEM((16, chunk_width), f32),
             pltpu.VMEM((16, chunk_width), f32),
-            pltpu.SemaphoreType.DMA((len(args),)),
+            pltpu.SemaphoreType.DMA((len(args) - 3 + 3 * local_experts,)),
             pltpu.SemaphoreType.DMA((5,)),
             pltpu.SemaphoreType.DMA((5,)),
         ],
@@ -401,6 +429,7 @@
         ),
         name="decode_layer",
     )(*args)
+    return hidden + routed
 
 
 def solution(mesh):

time: 27.2 us -> 25.8 us (0.949)
  local copies, waits for them, and re-layouts: 1.32 us -> 0 us
  other arithmetic: 0 us -> 0.62 us
  Pallas kernels: 25.6 us -> 25.1 us
    unnamed x1 -> x0, local copies, waits for them, and re-layouts: 1.32 us -> none
    add x0 -> x1, other arithmetic: none -> 0.62 us  [shards(): return hidden + routed]
    pallas_call x1, Pallas kernels: 25.6 us -> 25.1 us  [shards(): pl.pallas_call(functools.partial(kernel, G, H), out_shape=(part, part), i...]
where the time goes in v3:
time: 25.8 us; the launch traced here: 25.7 us
  Pallas kernels  25.1 us (97%)
  other arithmetic  0.62 us (2%)
    pallas_call x1, Pallas kernels, shards(): pl.pallas_call(functools.partial(kernel, G, H), out_shape=(part, part), i...  25.1 us
    add x1, other arithmetic, shards(): return hidden + routed  0.62 us

profile of v3, /device:TPU:0, one launch (start us, length us, event | category | flops | bytes accessed | tf_op | source)
XLA Modules:
  0.0 25.7 jit_solution(3478611899566642306)
XLA Ops:
  0.0 25.1 %decode_layer.1 = (f32[1,2,2048]{2,1,0:T(2,128)S(1)}, f32[1,2,2048]{2,1,0:T(2,128)S(1)}) custom-call(bf16[1,8,4096]{2,1,0:T(8,128)(2,1)} %q_hbm.1, bf16[1,128,512]{2,1,0:T(8,128)(2,1)} %k_hbm.1, bf16[1,128,512]{2,1,0:T(8,128)(2,1)} %v_hbm.1, bf16[1,2,16,512]{3,2,1,0:T(8,128)(2,1)} %sk_hbm.1, bf16[1,2,16,512]{3,2,1,0:T(8,128)(2,1)} %sv_hbm.1, ...), custom_call_target="tpu_custom_call" | custom-call | tf_op jit(solution)/shard_map/decode_layer/pallas_call | solution.py:404
  25.1 0.6 %add.3 = f32[1,2,2048]{2,1,0:T(2,128)} add(f32[1,2,2048]{2,1,0:T(2,128)S(1)} %get-tuple-element.7, f32[1,2,2048]{2,1,0:T(2,128)S(1)} %get-tuple-element.8) | non-fusion elementwise | flops 4096 | bytes 49152 | tf_op jit(solution)/shard_map/add | solution.py:432

commit v4 on v3

--- a/solution.py
+++ b/solution.py
@@ -126,7 +126,7 @@
             pairs.append((source.at[e], gu_ref.at[:, columns]))
         pairs.append((dw_hbm.at[e], dw_ref.at[pl.ds(e * hidden_units, hidden_units)]))
     loads = [pltpu.make_async_copy(a, b, load_sem.at[i]) for i, (a, b) in enumerate(pairs)]
-    for load in loads:
+    for load in loads[:9]:
         load.start()
 
     def other_group(i):
@@ -164,6 +164,7 @@
 
     for load in loads[:6]:
         load.wait()
+    loads[9].start()
     scale = 1.0 / math.sqrt(HEAD_SIZE)
     part = per_group * slot_rows
     count = G * part
@@ -233,6 +234,8 @@
             device_id=to,
             device_id_type=MESH,
         ).start()
+    for load in loads[10:]:
+        load.start()
     r1[g] = s1[g]
 
     for load in loads[6:9]:
@@ -261,7 +264,7 @@
         pltpu.make_async_copy(ref, ref, sem).wait()
 
     def to_peers(source, target, number):
-        for i in range(1, H):
+        for i in sorted(range(1, H), key=lambda i: abs(i - H // 2)):
             to = other_head(i)
             pltpu.make_async_remote_copy(
                 src_ref=source(to[1]),

time: 25.8 us -> 26 us (level)
  no operation moved by 1% of the time
where the time goes in v4:
time: 26 us; the launch traced here: 25.9 us
  Pallas kernels  25.2 us (97%)
  other arithmetic  0.62 us (2%)
    pallas_call x1, Pallas kernels, shards(): pl.pallas_call(functools.partial(kernel, G, H), out_shape=(part, part), i...  25.2 us
    add x1, other arithmetic, shards(): return hidden + routed  0.62 us

profile of v4, /device:TPU:0, one launch (start us, length us, event | category | flops | bytes accessed | tf_op | source)
XLA Modules:
  0.0 25.9 jit_solution(10661476063927764388)
XLA Ops:
  0.0 25.2 %decode_layer.1 = (f32[1,2,2048]{2,1,0:T(2,128)S(1)}, f32[1,2,2048]{2,1,0:T(2,128)S(1)}) custom-call(bf16[1,8,4096]{2,1,0:T(8,128)(2,1)} %q_hbm.1, bf16[1,128,512]{2,1,0:T(8,128)(2,1)} %k_hbm.1, bf16[1,128,512]{2,1,0:T(8,128)(2,1)} %v_hbm.1, bf16[1,2,16,512]{3,2,1,0:T(8,128)(2,1)} %sk_hbm.1, bf16[1,2,16,512]{3,2,1,0:T(8,128)(2,1)} %sv_hbm.1, ...), custom_call_target="tpu_custom_call" | custom-call | tf_op jit(solution)/shard_map/decode_layer/pallas_call | solution.py:407
  25.2 0.6 %add.3 = f32[1,2,2048]{2,1,0:T(2,128)} add(f32[1,2,2048]{2,1,0:T(2,128)S(1)} %get-tuple-element.7, f32[1,2,2048]{2,1,0:T(2,128)S(1)} %get-tuple-element.8) | non-fusion elementwise | flops 4096 | bytes 49152 | tf_op jit(solution)/shard_map/add | solution.py:435
